TPU v7x, 32 devices: a whole 2x2x4 slice. The times are simulated.
32 devices in a mesh: grp: 2 (over y), row: 4 (over z), col: 2 (over x), pair: 2 (over core).
Axes of the slice: x: 2, y: 2, z: 4, core: 2. Of those that a mesh axis runs over, the one named last changes fastest.
Arguments:
- features_in: bfloat16 [128, 32, 512], P('grp', 'row', ('col', 'pair')), parts along dimension 0, may hold values from -8 to 8
- filters_one: bfloat16 [64, 3, 3, 64], replicated, may hold values from -0.25 to 0.25
- filters_two: bfloat16 [512, 3, 3, 256], P('row'), may hold values from -0.125 to 0.125
- out_grad: bfloat16 [1024, 128, 8], P(('grp', 'row'), ('col', 'pair')), parts along dimension 0, may hold values from -24 to 24
Outputs:
- input_grad: bfloat16 [128, 32, 512], P('grp', 'row', ('col', 'pair')), parts along dimension 0
- grad_one: float32 [128, 3, 3, 64], P('grp'), parts along dimension 0
- grad_two: float32 [1024, 3, 3, 256], P(('grp', 'row')), parts along dimension 0
There are 2 independent parts, one for each index of `grp`. A program takes and returns all parts, laid end to end along the dimension named above; an argument that names none is the same for every part. Nothing has to cross between parts.
All inputs are finite; a program needn't handle non-finite values.
Results may differ from a plain program's by a relative error of at most 0.015.
Values may be sent and summed in bfloat16 or wider, within the bound.
A program may use at most 64 MiB of HBM per device.

v0:
```python
import math
import jax
import jax.numpy as jnp
from jax import lax
from jax.sharding import PartitionSpec as P


def padded_2(cells, sides, width):
    for axis, dim in sides:
        count = lax.axis_size(axis)
        ends = count - 1
        head = lax.slice_in_dim(cells, 0, width, axis=dim)
        tail = lax.slice_in_dim(cells, cells.shape[dim] - width, cells.shape[dim], axis=dim)
        cells = jnp.concatenate(
            [
                lax.ppermute(tail, axis, [(i, (i + 1) % count) for i in range(ends)]),
                cells,
                lax.ppermute(head, axis, [((i + 1) % count, i) for i in range(ends)]),
            ],
            axis=dim,
        )
    return cells


def conv_valid(padded, kernel):
    return lax.conv_general_dilated(
        padded[None],
        kernel,
        (1, 1),
        "VALID",
        dimension_numbers=("NCHW", "OHWI", "NCHW"),
        preferred_element_type=jnp.float32,
    )[0]


def flip_kernel(kernel):
    return jnp.transpose(kernel[:, ::-1, ::-1, :], (3, 1, 2, 0))


def silu_slope(values):
    sigmoid_value = jax.nn.sigmoid(values)
    return sigmoid_value * (1.0 + values * (1.0 - sigmoid_value))


def tap_grads(gradient, padded):
    row_count, col_count = (gradient.shape[1], gradient.shape[2])
    tap_list = []
    for first_tap in range(3):
        tap_row = []
        for second_tap in range(3):
            window = padded[
                :, first_tap : first_tap + row_count, second_tap : second_tap + col_count
            ]
            tap_row.append(
                jnp.einsum("ohw,chw->oc", gradient, window, preferred_element_type=jnp.float32)
            )
        tap_list.append(jnp.stack(tap_row, 1))
    return jnp.stack(tap_list, 1)


def pool_columns(active):
    channels, row_count, col_count = active.shape
    folded = active.reshape(channels, row_count // 4, 2, 2, col_count // 4, 2, 2).mean(axis=(3, 6))
    return jnp.transpose(folded, (0, 2, 4, 3, 1)).reshape(
        channels * 4, col_count // 4, row_count // 4
    )


def unpool_columns(gradient):
    quad_count, col_count, row_count = gradient.shape
    ordered = jnp.transpose(
        gradient.reshape(quad_count // 4, 2, 2, col_count, row_count), (0, 4, 1, 3, 2)
    )
    spread = (
        jnp.broadcast_to(
            ordered[:, :, :, None, :, :, None], (quad_count // 4, row_count, 2, 2, col_count, 2, 2)
        )
        * 0.25
    )
    return spread.reshape(quad_count // 4, row_count * 4, col_count * 4)


def local(features_in, filters_one, filters_two, out_grad):
    band_rows = features_in.shape[1]
    strip_cols = features_in.shape[2]
    height = band_rows * lax.axis_size("row")
    width = strip_cols * lax.axis_size(("col", "pair"))
    padded_in = padded_2(features_in, (("row", 1), (("col", "pair"), 2)), 1)
    pre_one = conv_valid(padded_in, filters_one)
    pooled = pool_columns(jax.nn.silu(pre_one)).astype(jnp.bfloat16)
    with_edges = padded_2(pooled, ((("col", "pair"), 1),), 1)
    column_strip = lax.all_gather(with_edges, "row", axis=2, tiled=True)
    strip_padded = jnp.pad(column_strip, ((0, 0), (0, 0), (1, 1)))
    swapped = jnp.transpose(filters_two, (0, 2, 1, 3))
    pre_two = conv_valid(strip_padded, swapped)
    grad_pre_two = (out_grad.astype(jnp.float32) * silu_slope(pre_two)).astype(jnp.bfloat16)
    pooled_height = column_strip.shape[2]
    pooled_width = strip_cols // 4 * lax.axis_size(("col", "pair"))
    local_two = jnp.transpose(tap_grads(grad_pre_two, strip_padded), (0, 2, 1, 3))
    grad_two = lax.psum(local_two, ("col", "pair")) / math.sqrt(pooled_height * pooled_width)
    padded_grad = jnp.pad(grad_pre_two, ((0, 0), (2, 2), (1, 1)))
    spread_grad = conv_valid(padded_grad, flip_kernel(swapped))
    with_ghosts = padded_2(spread_grad, ((("col", "pair"), 1),), 1)
    real_columns = spread_grad[:, 1:-1, :]
    real_columns = real_columns.at[:, 0, :].add(with_ghosts[:, 0, :])
    real_columns = real_columns.at[:, -1, :].add(with_ghosts[:, -1, :])
    grad_pooled = lax.psum_scatter(real_columns, "row", scatter_dimension=2, tiled=True)
    grad_pre_one = (unpool_columns(grad_pooled) * silu_slope(pre_one)).astype(jnp.bfloat16)
    local_one = tap_grads(grad_pre_one, padded_in)
    grad_one = lax.psum(local_one, ("row", "col", "pair")) / math.sqrt(height * width)
    rimmed_one = padded_2(grad_pre_one, (("row", 1), (("col", "pair"), 2)), 1)
    input_grad = conv_valid(rimmed_one, flip_kernel(filters_one)).astype(jnp.bfloat16)
    return (input_grad, grad_one, grad_two)


def solution(mesh):
    in_specs = (
        P("grp", "row", ("col", "pair")),
        P(),
        P("row", None, None, None),
        P(("grp", "row"), ("col", "pair"), None),
    )
    out_specs = (
        P("grp", "row", ("col", "pair")),
        P("grp", None, None, None),
        P(("grp", "row"), None, None, None),
    )
    return jax.shard_map(local, mesh=mesh, in_specs=in_specs, out_specs=out_specs, check_vma=False)
```

profile of v0, /device:TPU:0, one launch (start us, length us, event | category | flops | bytes accessed | tf_op | source)
XLA Modules:
  0.0 211.8 jit_solution(14888131075437018906)
XLA Ops:
  8.1 1.0 copy.216
  9.1 4.9 %collective-permute-start = (bf16[64,1,128]{2,0,1:T(8,128)(2,1)S(1)}, bf16[64,1,128]{2,0,1:T(8,128)(2,1)S(1)}, u32[]{:S(2)}, u32[]{:S(2)}) collective-permute-start(bf16[64,1,128]{2,0,1:T(8,128)(2,1)S(1)} %get-tuple-element.58), channel_id=1, source_target_pairs={{0,4},{4,8},{8,12},{1,5},{5,9},{9,13},{2,6},{6,10},{10,14},{3,7},{... | collective-permute-start | bytes 49160 | tf_op jit(solution)/shard_map/ppermute | solution.py:16
  14.0 1.3 collective-permute-start.1
  15.4 0.9 constant_dynamic-update-slice_fusion.1
  16.4 3.3 %collective-permute-done.1 = bf16[64,1,128]{2,0,1:T(8,128)(2,1)S(1)} collective-permute-done((bf16[64,1,128]{2,0,1:T(8,128)(2,1)S(1)}, bf16[64,1,128]{2,0,1:T(8,128)(2,1)S(1)}, u32[]{:S(2)}, u32[]{:S(2)}) %collective-permute-start.1) | collective-permute-done | bytes 16416 | tf_op jit(solution)/shard_map/ppermute | solution.py:18
  19.7 1.3 collective-permute-start.3
  21.0 3.0 %collective-permute-start.2 = (bf16[64,10,1]{2,0,1:T(8,128)(2,1)S(1)}, bf16[64,10,1]{2,0,1:T(8,128)(2,1)S(1)}, u32[]{:S(2)}, u32[]{:S(2)}) collective-permute-start(bf16[64,10,1]{2,0,1:T(8,128)(2,1)S(1)} %get-tuple-element.51), channel_id=1, source_target_pairs={{0,1},{1,2},{2,3},{4,5},{5,6},{6,7},{8,9},{9,10},{10,11},{12,13},{... | collective-permute-start | bytes 3848 | tf_op jit(solution)/shard_map/ppermute | solution.py:16
  24.1 1.0 collective-permute-done.2
  25.1 0.2 maximum_bitcast_fusion.4
  25.3 0.3 copy.265
  25.9 0.6 copy-done.3
  26.5 0.8 convolution_select_fusion.1
  27.6 0.9 fusion.3
  28.8 1.3 collective-permute-start.5
  30.1 4.9 %collective-permute-start.4 = (bf16[256,1,2]{1,0,2:T(8,128)(2,1)S(1)}, bf16[256,1,2]{1,0,2:T(8,128)(2,1)S(1)}, u32[]{:S(2)}, u32[]{:S(2)}) collective-permute-start(bf16[256,1,2]{1,0,2:T(8,128)(2,1)S(1)} %get-tuple-element.55), channel_id=1, source_target_pairs={{0,1},{1,2},{2,3},{4,5},{5,6},{6,7},{8,9},{9,10},{10,11},{12,13},{... | collective-permute-start | bytes 3080 | tf_op jit(solution)/shard_map/ppermute | solution.py:16
  35.0 0.2 copy.264
  35.3 0.7 collective-permute-done.4
  36.0 0.1 pad_maximum_fusion.9
  36.2 13.7 %all_gather.3 = bf16[256,34,8]{0,1,2:T(8,128)(2,1)S(1)} all-gather(bf16[256,34,2]{0,1,2:T(8,128)(2,1)S(1)} %copy.226), channel_id=1, replica_groups=mesh['grp'=2,'row'=4,'col'=2,'pair'=2] {'row'}, dimensions={2}, use_global_device_ids=true | all-gather | bytes 174080 | tf_op jit(solution)/shard_map/all_gather | solution.py:92
  50.1 1.0 fusion.6
  51.3 0.2 convolution_bitcast_fusion
  51.5 0.2 convolution_bitcast_fusion.1
  51.7 0.2 convolution_bitcast_fusion.2
  51.9 0.2 convolution_bitcast_fusion.6
  52.1 0.2 convolution_bitcast_fusion.7
  52.4 0.2 convolution_bitcast_fusion.8
  52.6 0.2 convolution_bitcast_fusion.3
  52.8 1.0 fusion.4
  53.9 2.4 %collective-permute-start.6 = (f32[256,1,8]{0,2,1:T(8,128)S(1)}, f32[256,1,8]{0,2,1:T(8,128)S(1)}, u32[]{:S(2)}, u32[]{:S(2)}) collective-permute-start(f32[256,1,8]{0,2,1:T(8,128)S(1)} %get-tuple-element.48), channel_id=1, source_target_pairs={{0,1},{1,2},{2,3},{4,5},{5,6},{6,7},{8,9},{9,10},{10,11},{12,13},{... | collective-permute-start | bytes 24584 | tf_op jit(solution)/shard_map/ppermute | solution.py:16
  56.3 0.2 convolution_bitcast_fusion.5
  56.6 1.3 collective-permute-start.7
  57.9 6.6 %collective-permute-done.7 = f32[256,1,8]{0,2,1:T(8,128)S(1)} collective-permute-done((f32[256,1,8]{0,2,1:T(8,128)S(1)}, f32[256,1,8]{0,2,1:T(8,128)S(1)}, u32[]{:S(2)}, u32[]{:S(2)}) %collective-permute-start.7) | collective-permute-done | bytes 8224 | tf_op jit(solution)/shard_map/ppermute | solution.py:18
  64.4 0.8 copy.233
  65.3 0.2 convolution_bitcast_fusion.4
  65.7 1.1 maximum_bitcast_fusion
  66.8 18.7 %reduce-scatter.2.cloned.1.call-done = f32[256,32,2]{0,1,2:T(8,128)} async-done(((f32[256,32,8]{0,1,2:T(8,128)}), f32[256,32,2]{0,1,2:T(8,128)}) %reduce-scatter.2.cloned.1.call-update) | async-done | bytes 65552 | tf_op jit(solution)/shard_map/reduce_scatter | solution.py:107
  85.5 0.8 broadcast_multiply_fusion.2
  86.8 0.2 copy.236
  87.1 0.4 copy-done.1
  87.5 0.2 convolution_bitcast_fusion.13
  87.7 1.3 collective-permute-start.8
  89.0 1.3 collective-permute-start.9
  90.3 0.3 convolution_bitcast_fusion.15
  90.6 0.2 convolution_bitcast_fusion.16
  90.8 0.3 convolution_bitcast_fusion.17
  91.0 0.3 convolution_bitcast_fusion.12
  91.3 0.3 convolution_bitcast_fusion.14
  91.6 0.3 convolution_bitcast_fusion.9
  91.9 0.2 convolution_bitcast_fusion.10
  92.0 0.2 convolution_bitcast_fusion.11
  92.4 2.4 %collective-permute-done.9 = bf16[64,1,128]{2,1,0:T(2,128)(2,1)S(1)} collective-permute-done((bf16[64,1,128]{2,1,0:T(2,128)(2,1)S(1)}, bf16[64,1,128]{2,1,0:T(2,128)(2,1)S(1)}, u32[]{:S(2)}, u32[]{:S(2)}) %collective-permute-start.9) | collective-permute-done | bytes 16416 | tf_op jit(solution)/shard_map/ppermute | solution.py:18
  94.9 1.3 collective-permute-start.11
  96.2 3.0 %collective-permute-start.10 = (bf16[64,10,1]{2,0,1:T(8,128)(2,1)S(1)}, bf16[64,10,1]{2,0,1:T(8,128)(2,1)S(1)}, u32[]{:S(2)}, u32[]{:S(2)}) collective-permute-start(bf16[64,10,1]{2,0,1:T(8,128)(2,1)S(1)} %get-tuple-element.49), channel_id=1, source_target_pairs={{0,1},{1,2},{2,3},{4,5},{5,6},{6,7},{8,9},{9,10},{10,11},{12,13},{... | collective-permute-start | bytes 3848 | tf_op jit(solution)/shard_map/ppermute | solution.py:16
  99.3 0.7 pad_maximum_fusion
  100.0 0.2 collective-permute-done.10
  100.3 0.2 maximum_bitcast_fusion.5
  100.5 0.3 copy.266
  101.0 0.6 fusion
  101.7 0.9 copy.259
  102.6 5.7 %all-reduce.7.cloned.1.call-done = f32[128,3,3,256]{3,0,1,2:T(8,128)} async-done(((f32[128,3,3,256]{3,0,1,2:T(8,128)}), f32[128,3,3,256]{3,0,1,2:T(8,128)}) %all-reduce.7.cloned.1.call-update) | async-done | bytes 1179664 | tf_op jit(solution)/shard_map/psum | solution.py:100
  108.3 1.4 broadcast_multiply_fusion
  109.7 1.1 copy.260
  110.8 91.9 %all-reduce.5.cloned.1.call-done = f32[64,3,3,64]{3,0,2,1:T(8,128)} async-done(((f32[64,3,3,64]{3,0,2,1:T(8,128)}), f32[64,3,3,64]{3,0,2,1:T(8,128)}) %all-reduce.5.cloned.1.call-update) | async-done | bytes 147472 | tf_op jit(solution)/shard_map/psum | solution.py:110
  202.6 1.7 broadcast_multiply_fusion.1
  (63 shorter events, 2.9 us)
Async XLA Ops:
  8.0 42.1 %copy-start = (bf16[128,3,3,256]{3,0,2,1:T(8,128)(2,1)S(1)}, bf16[128,3,3,256]{3,0,2,1:T(8,128)(2,1)}, u32[]{:S(2)}) copy-start(bf16[128,3,3,256]{3,0,2,1:T(8,128)(2,1)} %param.10) | copy-start | bytes 1769476
  8.0 77.5 %reduce-scatter.2.cloned.1.call-start = ((), (), s32[]{:S(2)}) async-start(), calls=%async_computation.1 | async-start | bytes 327680 | tf_op jit(solution)/shard_map/reduce_scatter | solution.py:107
  9.1 6.4 %collective-permute-start = (bf16[64,1,128]{2,0,1:T(8,128)(2,1)S(1)}, bf16[64,1,128]{2,0,1:T(8,128)(2,1)S(1)}, u32[]{:S(2)}, u32[]{:S(2)}) collective-permute-start(bf16[64,1,128]{2,0,1:T(8,128)(2,1)S(1)} %get-tuple-element.58), channel_id=1, source_target_pairs={{0,4},{4,8},{8,12},{1,5},{5,9},{9,13},{2,6},{6,10},{10,14},{3,7},{... | collective-permute-start | bytes 49160 | tf_op jit(solution)/shard_map/ppermute | solution.py:16
  14.0 5.6 %collective-permute-start.1 = (bf16[64,1,128]{2,0,1:T(8,128)(2,1)S(1)}, bf16[64,1,128]{2,0,1:T(8,128)(2,1)S(1)}, u32[]{:S(2)}, u32[]{:S(2)}) collective-permute-start(bf16[64,1,128]{2,0,1:T(8,128)(2,1)S(1)} %get-tuple-element.57), channel_id=1, source_target_pairs={{4,0},{8,4},{12,8},{5,1},{9,5},{13,9},{6,2},{10,6},{14,10},{7,3},{... | collective-permute-start | bytes 49160 | tf_op jit(solution)/shard_map/ppermute | solution.py:18
  19.7 4.4 %collective-permute-start.3 = (bf16[64,10,1]{2,0,1:T(8,128)(2,1)S(1)}, bf16[64,10,1]{2,0,1:T(8,128)(2,1)S(1)}, u32[]{:S(2)}, u32[]{:S(2)}) collective-permute-start(bf16[64,10,1]{2,0,1:T(8,128)(2,1)S(1)} %get-tuple-element.52), channel_id=1, source_target_pairs={{1,0},{2,1},{3,2},{5,4},{6,5},{7,6},{9,8},{10,9},{11,10},{13,12},{... | collective-permute-start | bytes 3848 | tf_op jit(solution)/shard_map/ppermute | solution.py:18
  21.0 4.0 %collective-permute-start.2 = (bf16[64,10,1]{2,0,1:T(8,128)(2,1)S(1)}, bf16[64,10,1]{2,0,1:T(8,128)(2,1)S(1)}, u32[]{:S(2)}, u32[]{:S(2)}) collective-permute-start(bf16[64,10,1]{2,0,1:T(8,128)(2,1)S(1)} %get-tuple-element.51), channel_id=1, source_target_pairs={{0,1},{1,2},{2,3},{4,5},{5,6},{6,7},{8,9},{9,10},{10,11},{12,13},{... | collective-permute-start | bytes 3848 | tf_op jit(solution)/shard_map/ppermute | solution.py:16
  25.6 0.9 copy-start.3
  25.6 0.9 copy-start.4
  28.8 6.4 %collective-permute-start.5 = (bf16[256,1,2]{1,0,2:T(8,128)(2,1)S(1)}, bf16[256,1,2]{1,0,2:T(8,128)(2,1)S(1)}, u32[]{:S(2)}, u32[]{:S(2)}) collective-permute-start(bf16[256,1,2]{1,0,2:T(8,128)(2,1)S(1)} %get-tuple-element.56), channel_id=1, source_target_pairs={{1,0},{2,1},{3,2},{5,4},{6,5},{7,6},{9,8},{10,9},{11,10},{13,12},{... | collective-permute-start | bytes 3080 | tf_op jit(solution)/shard_map/ppermute | solution.py:18
  30.1 5.9 %collective-permute-start.4 = (bf16[256,1,2]{1,0,2:T(8,128)(2,1)S(1)}, bf16[256,1,2]{1,0,2:T(8,128)(2,1)S(1)}, u32[]{:S(2)}, u32[]{:S(2)}) collective-permute-start(bf16[256,1,2]{1,0,2:T(8,128)(2,1)S(1)} %get-tuple-element.55), channel_id=1, source_target_pairs={{0,1},{1,2},{2,3},{4,5},{5,6},{6,7},{8,9},{9,10},{10,11},{12,13},{... | collective-permute-start | bytes 3080 | tf_op jit(solution)/shard_map/ppermute | solution.py:16
  50.1 1.0 copy-start.2
  53.9 4.0 %collective-permute-start.6 = (f32[256,1,8]{0,2,1:T(8,128)S(1)}, f32[256,1,8]{0,2,1:T(8,128)S(1)}, u32[]{:S(2)}, u32[]{:S(2)}) collective-permute-start(f32[256,1,8]{0,2,1:T(8,128)S(1)} %get-tuple-element.48), channel_id=1, source_target_pairs={{0,1},{1,2},{2,3},{4,5},{5,6},{6,7},{8,9},{9,10},{10,11},{12,13},{... | collective-permute-start | bytes 24584 | tf_op jit(solution)/shard_map/ppermute | solution.py:16
  56.6 7.9 %collective-permute-start.7 = (f32[256,1,8]{0,2,1:T(8,128)S(1)}, f32[256,1,8]{0,2,1:T(8,128)S(1)}, u32[]{:S(2)}, u32[]{:S(2)}) collective-permute-start(f32[256,1,8]{0,2,1:T(8,128)S(1)} %get-tuple-element.47), channel_id=1, source_target_pairs={{1,0},{2,1},{3,2},{5,4},{6,5},{7,6},{9,8},{10,9},{11,10},{13,12},{... | collective-permute-start | bytes 24584 | tf_op jit(solution)/shard_map/ppermute | solution.py:18
  65.3 43.0 %all-reduce.7.cloned.1.call-start = ((), (), s32[]{:S(2)}) async-start(), calls=%async_computation.3 | async-start | bytes 2359296 | tf_op jit(solution)/shard_map/psum | solution.py:100
  66.8 135.9 %all-reduce.5.cloned.1.call-start = ((), (), s32[]{:S(2)}) async-start(), calls=%async_computation.2 | async-start | bytes 589824 | tf_op jit(solution)/shard_map/psum | solution.py:110
  86.6 0.9 copy-start.1
  87.7 4.6 %collective-permute-start.8 = (bf16[64,1,128]{2,1,0:T(2,128)(2,1)S(1)}, bf16[64,1,128]{2,1,0:T(2,128)(2,1)S(1)}, u32[]{:S(2)}, u32[]{:S(2)}) collective-permute-start(bf16[64,1,128]{2,1,0:T(2,128)(2,1)S(1)} %get-tuple-element.54), channel_id=1, source_target_pairs={{0,4},{4,8},{8,12},{1,5},{5,9},{9,13},{2,6},{6,10},{10,14},{3,7},{... | collective-permute-start | bytes 49160 | tf_op jit(solution)/shard_map/ppermute | solution.py:16
  89.0 5.8 %collective-permute-start.9 = (bf16[64,1,128]{2,1,0:T(2,128)(2,1)S(1)}, bf16[64,1,128]{2,1,0:T(2,128)(2,1)S(1)}, u32[]{:S(2)}, u32[]{:S(2)}) collective-permute-start(bf16[64,1,128]{2,1,0:T(2,128)(2,1)S(1)} %get-tuple-element.53), channel_id=1, source_target_pairs={{4,0},{8,4},{12,8},{5,1},{9,5},{13,9},{6,2},{10,6},{14,10},{7,3},{... | collective-permute-start | bytes 49160 | tf_op jit(solution)/shard_map/ppermute | solution.py:18
  94.9 5.1 %collective-permute-start.11 = (bf16[64,10,1]{2,0,1:T(8,128)(2,1)S(1)}, bf16[64,10,1]{2,0,1:T(8,128)(2,1)S(1)}, u32[]{:S(2)}, u32[]{:S(2)}) collective-permute-start(bf16[64,10,1]{2,0,1:T(8,128)(2,1)S(1)} %get-tuple-element.50), channel_id=1, source_target_pairs={{1,0},{2,1},{3,2},{5,4},{6,5},{7,6},{9,8},{10,9},{11,10},{13,12},{... | collective-permute-start | bytes 3848 | tf_op jit(solution)/shard_map/ppermute | solution.py:18
  96.2 4.0 %collective-permute-start.10 = (bf16[64,10,1]{2,0,1:T(8,128)(2,1)S(1)}, bf16[64,10,1]{2,0,1:T(8,128)(2,1)S(1)}, u32[]{:S(2)}, u32[]{:S(2)}) collective-permute-start(bf16[64,10,1]{2,0,1:T(8,128)(2,1)S(1)} %get-tuple-element.49), channel_id=1, source_target_pairs={{0,1},{1,2},{2,3},{4,5},{5,6},{6,7},{8,9},{9,10},{10,11},{12,13},{... | collective-permute-start | bytes 3848 | tf_op jit(solution)/shard_map/ppermute | solution.py:16
Sparse Core Ops, SparseCore 0:
  65.4 20.0 reduce-scatter.1
Sparse Core Ops, SparseCore 1:
  68.8 39.4 all-reduce.6
  112.5 90.1 all-reduce.4
where the time goes:
time: 212 us
  waiting for transfers between devices  131 us (62%)
  starting transfers between devices  27.5 us (13%)
  between operations  16.1 us (8%)
  blocking collectives  13.7 us (6%)
  local copies, waits for them, and re-layouts  8.75 us (4%)
  other arithmetic  7.58 us (4%)
  matrix products  7.49 us (4%)
    psum x1, waiting for transfers between devices, local(): lax.psum(local_one, ('row', 'col', 'pair')) / math.sqrt(height * width)  91.9 us
    ppermute x6, starting transfers between devices, padded_2(): lax.ppermute(tail, axis, [(i, (i + 1) % count) for i in range(ends)])  19.6 us
    reduce_scatter x1, waiting for transfers between devices, local(): lax.psum_scatter(real_columns, 'row', scatter_dimension=2, tiled=True)  18.7 us
    all_gather x1, blocking collectives, local(): column_strip = lax.all_gather(with_edges, 'row', axis=2, tiled=True)  13.7 us
    ppermute x6, waiting for transfers between devices, padded_2(): lax.ppermute(head, axis, [((i + 1) % count, i) for i in range(ends)])  12.2 us
    ppermute x6, starting transfers between devices, padded_2(): lax.ppermute(head, axis, [((i + 1) % count, i) for i in range(ends)])  7.75 us
    psum x1, waiting for transfers between devices, local(): lax.psum(local_two, ('col', 'pair'))  5.73 us
    unnamed x21, local copies, waits for them, and re-layouts  5.7 us
  transfers between devices with their start and end apart: 15, of which 10 were waited for; matrix products, arithmetic and copies ran while one was open for 6% of the time, Pallas kernels for 0%

commit v1 on v0

--- a/solution.py
+++ b/solution.py
@@ -107,7 +107,7 @@
     grad_pooled = lax.psum_scatter(real_columns, "row", scatter_dimension=2, tiled=True)
     grad_pre_one = (unpool_columns(grad_pooled) * silu_slope(pre_one)).astype(jnp.bfloat16)
     local_one = tap_grads(grad_pre_one, padded_in)
-    grad_one = lax.psum(local_one, ("row", "col", "pair")) / math.sqrt(height * width)
+    grad_one = lax.psum(lax.psum(local_one, ("col", "pair")), "row") / math.sqrt(height * width)
     rimmed_one = padded_2(grad_pre_one, (("row", 1), (("col", "pair"), 2)), 1)
     input_grad = conv_valid(rimmed_one, flip_kernel(filters_one)).astype(jnp.bfloat16)
     return (input_grad, grad_one, grad_two)

time: 212 us -> 184 us (0.87)
  waiting for transfers between devices: 131 us -> 104 us
    psum x2, waiting for transfers between devices: 97.6 us -> 70.4 us  [the longest x1 35.8 us: local(): lax.psum(lax.psum(local_one, ('col', 'pair')), 'row')]
where the time goes in v1:
time: 184 us; the launch traced here: 183 us
  waiting for transfers between devices  104 us (57%)
  starting transfers between devices  27.5 us (15%)
  between operations  14.4 us (8%)
  blocking collectives  13.7 us (7%)
  local copies, waits for them, and re-layouts  8.75 us (5%)
  other arithmetic  7.59 us (4%)
  matrix products  7.48 us (4%)
    psum x1, waiting for transfers between devices, local(): lax.psum(lax.psum(local_one, ('col', 'pair')), 'row')  35.8 us
    psum x1, waiting for transfers between devices, local(): lax.psum(local_one, ('col', 'pair'))  34.5 us
    ppermute x6, starting transfers between devices, padded_2(): lax.ppermute(tail, axis, [(i, (i + 1) % count) for i in range(ends)])  19.6 us
    reduce_scatter x1, waiting for transfers between devices, local(): lax.psum_scatter(real_columns, 'row', scatter_dimension=2, tiled=True)  18.8 us
    all_gather x1, blocking collectives, local(): column_strip = lax.all_gather(with_edges, 'row', axis=2, tiled=True)  13.7 us
    ppermute x6, waiting for transfers between devices, padded_2(): lax.ppermute(head, axis, [((i + 1) % count, i) for i in range(ends)])  11.4 us
    ppermute x6, starting transfers between devices, padded_2(): lax.ppermute(head, axis, [((i + 1) % count, i) for i in range(ends)])  7.75 us
    unnamed x21, local copies, waits for them, and re-layouts  5.7 us
  transfers between devices with their start and end apart: 15, of which 10 were waited for; matrix products, arithmetic and copies ran while one was open for 6% of the time, Pallas kernels for 0%

profile of v1, /device:TPU:0, one launch (start us, length us, event | category | flops | bytes accessed | tf_op | source)
XLA Modules:
  0.0 183.0 jit_solution(10919358876482067859)
XLA Ops:
  7.2 1.0 copy.216
  8.2 4.9 %collective-permute-start = (bf16[64,1,128]{2,0,1:T(8,128)(2,1)S(1)}, bf16[64,1,128]{2,0,1:T(8,128)(2,1)S(1)}, u32[]{:S(2)}, u32[]{:S(2)}) collective-permute-start(bf16[64,1,128]{2,0,1:T(8,128)(2,1)S(1)} %get-tuple-element.60), channel_id=1, source_target_pairs={{0,4},{4,8},{8,12},{1,5},{5,9},{9,13},{2,6},{6,10},{10,14},{3,7},{... | collective-permute-start | bytes 49160 | tf_op jit(solution)/shard_map/ppermute | solution.py:16
  13.2 1.3 collective-permute-start.1
  14.6 0.9 constant_dynamic-update-slice_fusion.1
  15.5 3.3 %collective-permute-done.1 = bf16[64,1,128]{2,0,1:T(8,128)(2,1)S(1)} collective-permute-done((bf16[64,1,128]{2,0,1:T(8,128)(2,1)S(1)}, bf16[64,1,128]{2,0,1:T(8,128)(2,1)S(1)}, u32[]{:S(2)}, u32[]{:S(2)}) %collective-permute-start.1) | collective-permute-done | bytes 16416 | tf_op jit(solution)/shard_map/ppermute | solution.py:18
  18.9 1.3 collective-permute-start.3
  20.2 3.0 %collective-permute-start.2 = (bf16[64,10,1]{2,0,1:T(8,128)(2,1)S(1)}, bf16[64,10,1]{2,0,1:T(8,128)(2,1)S(1)}, u32[]{:S(2)}, u32[]{:S(2)}) collective-permute-start(bf16[64,10,1]{2,0,1:T(8,128)(2,1)S(1)} %get-tuple-element.53), channel_id=1, source_target_pairs={{0,1},{1,2},{2,3},{4,5},{5,6},{6,7},{8,9},{9,10},{10,11},{12,13},{... | collective-permute-start | bytes 3848 | tf_op jit(solution)/shard_map/ppermute | solution.py:16
  23.3 1.0 collective-permute-done.2
  24.3 0.2 maximum_bitcast_fusion.4
  24.5 0.3 copy.265
  25.1 0.6 copy-done.3
  25.7 0.8 convolution_select_fusion.1
  26.8 0.9 fusion.3
  28.0 1.3 collective-permute-start.5
  29.3 4.9 %collective-permute-start.4 = (bf16[256,1,2]{1,0,2:T(8,128)(2,1)S(1)}, bf16[256,1,2]{1,0,2:T(8,128)(2,1)S(1)}, u32[]{:S(2)}, u32[]{:S(2)}) collective-permute-start(bf16[256,1,2]{1,0,2:T(8,128)(2,1)S(1)} %get-tuple-element.57), channel_id=1, source_target_pairs={{0,1},{1,2},{2,3},{4,5},{5,6},{6,7},{8,9},{9,10},{10,11},{12,13},{... | collective-permute-start | bytes 3080 | tf_op jit(solution)/shard_map/ppermute | solution.py:16
  34.2 0.2 copy.264
  34.4 0.7 collective-permute-done.4
  35.1 0.1 pad_maximum_fusion.9
  35.4 13.7 %all_gather.3 = bf16[256,34,8]{0,1,2:T(8,128)(2,1)S(1)} all-gather(bf16[256,34,2]{0,1,2:T(8,128)(2,1)S(1)} %copy.226), channel_id=1, replica_groups=mesh['grp'=2,'row'=4,'col'=2,'pair'=2] {'row'}, dimensions={2}, use_global_device_ids=true | all-gather | bytes 174080 | tf_op jit(solution)/shard_map/all_gather | solution.py:92
  49.3 1.0 fusion.6
  50.4 0.2 convolution_bitcast_fusion
  50.6 0.2 convolution_bitcast_fusion.1
  50.9 0.2 convolution_bitcast_fusion.2
  51.1 0.2 convolution_bitcast_fusion.6
  51.3 0.2 convolution_bitcast_fusion.7
  51.5 0.2 convolution_bitcast_fusion.8
  51.7 0.2 convolution_bitcast_fusion.3
  52.0 1.0 fusion.4
  53.0 2.4 %collective-permute-start.6 = (f32[256,1,8]{0,2,1:T(8,128)S(1)}, f32[256,1,8]{0,2,1:T(8,128)S(1)}, u32[]{:S(2)}, u32[]{:S(2)}) collective-permute-start(f32[256,1,8]{0,2,1:T(8,128)S(1)} %get-tuple-element.50), channel_id=1, source_target_pairs={{0,1},{1,2},{2,3},{4,5},{5,6},{6,7},{8,9},{9,10},{10,11},{12,13},{... | collective-permute-start | bytes 24584 | tf_op jit(solution)/shard_map/ppermute | solution.py:16
  55.5 0.2 convolution_bitcast_fusion.5
  55.7 1.3 collective-permute-start.7
  57.0 6.6 %collective-permute-done.7 = f32[256,1,8]{0,2,1:T(8,128)S(1)} collective-permute-done((f32[256,1,8]{0,2,1:T(8,128)S(1)}, f32[256,1,8]{0,2,1:T(8,128)S(1)}, u32[]{:S(2)}, u32[]{:S(2)}) %collective-permute-start.7) | collective-permute-done | bytes 8224 | tf_op jit(solution)/shard_map/ppermute | solution.py:18
  63.6 0.8 copy.233
  64.5 0.2 convolution_bitcast_fusion.4
  64.8 1.1 maximum_bitcast_fusion
  65.9 18.8 %reduce-scatter.2.cloned.1.call-done = f32[256,32,2]{0,1,2:T(8,128)} async-done(((f32[256,32,8]{0,1,2:T(8,128)}), f32[256,32,2]{0,1,2:T(8,128)}) %reduce-scatter.2.cloned.1.call-update) | async-done | bytes 65552 | tf_op jit(solution)/shard_map/reduce_scatter | solution.py:107
  84.7 0.8 broadcast_multiply_fusion.2
  86.0 0.2 copy.236
  86.4 0.4 copy-done.1
  86.7 0.2 convolution_bitcast_fusion.13
  86.9 1.3 collective-permute-start.8
  88.2 1.3 collective-permute-start.9
  89.5 0.3 convolution_bitcast_fusion.9
  89.8 0.2 convolution_bitcast_fusion.10
  90.0 0.2 convolution_bitcast_fusion.11
  90.3 0.3 convolution_bitcast_fusion.15
  90.5 0.2 convolution_bitcast_fusion.16
  90.7 0.2 convolution_bitcast_fusion.17
  91.0 0.3 convolution_bitcast_fusion.12
  91.3 0.3 convolution_bitcast_fusion.14
  91.6 0.7 pad_maximum_fusion
  92.4 1.6 collective-permute-done.9
  94.2 1.3 collective-permute-start.11
  95.5 3.0 %collective-permute-start.10 = (bf16[64,10,1]{2,0,1:T(8,128)(2,1)S(1)}, bf16[64,10,1]{2,0,1:T(8,128)(2,1)S(1)}, u32[]{:S(2)}, u32[]{:S(2)}) collective-permute-start(bf16[64,10,1]{2,0,1:T(8,128)(2,1)S(1)} %get-tuple-element.51), channel_id=1, source_target_pairs={{0,1},{1,2},{2,3},{4,5},{5,6},{6,7},{8,9},{9,10},{10,11},{12,13},{... | collective-permute-start | bytes 3848 | tf_op jit(solution)/shard_map/ppermute | solution.py:16
  98.5 1.2 collective-permute-done.10
  99.7 0.2 maximum_bitcast_fusion.5
  99.9 0.3 copy.266
  100.4 0.6 fusion
  101.1 0.9 copy.259
  102.0 34.5 %all-reduce.8.cloned.1.call-done = (f32[64,3,3,64]{3,0,2,1:T(8,128)}, f32[128,3,3,256]{3,0,1,2:T(8,128)}) async-done(((f32[64,3,3,64]{3,0,2,1:T(8,128)}, f32[128,3,3,256]{3,0,1,2:T(8,128)}), (f32[64,3,3,64]{3,0,2,1:T(8,128)}, f32[128,3,3,256]{3,0,1,2:T(8,128)})) %all-reduce.8.cloned.1.call-update) | async-done | bytes 1327120 | tf_op jit(solution)/shard_map/psum | solution.py:110
  136.5 1.4 broadcast_multiply_fusion
  137.9 1.1 copy.260
  139.0 35.8 %all-reduce.6.cloned.1.call-done = f32[64,3,3,64]{3,0,2,1:T(8,128)} async-done(((f32[64,3,3,64]{3,0,2,1:T(8,128)}), f32[64,3,3,64]{3,0,2,1:T(8,128)}) %all-reduce.6.cloned.1.call-update) | async-done | bytes 147472 | tf_op jit(solution)/shard_map/psum | solution.py:110
  174.8 1.7 broadcast_multiply_fusion.1
  (63 shorter events, 2.9 us)
Async XLA Ops:
  7.2 42.1 %copy-start = (bf16[128,3,3,256]{3,0,2,1:T(8,128)(2,1)S(1)}, bf16[128,3,3,256]{3,0,2,1:T(8,128)(2,1)}, u32[]{:S(2)}) copy-start(bf16[128,3,3,256]{3,0,2,1:T(8,128)(2,1)} %param.10) | copy-start | bytes 1769476
  7.2 77.5 %reduce-scatter.2.cloned.1.call-start = ((), (), s32[]{:S(2)}) async-start(), calls=%async_computation.1 | async-start | bytes 327680 | tf_op jit(solution)/shard_map/reduce_scatter | solution.py:107
  8.2 6.4 %collective-permute-start = (bf16[64,1,128]{2,0,1:T(8,128)(2,1)S(1)}, bf16[64,1,128]{2,0,1:T(8,128)(2,1)S(1)}, u32[]{:S(2)}, u32[]{:S(2)}) collective-permute-start(bf16[64,1,128]{2,0,1:T(8,128)(2,1)S(1)} %get-tuple-element.60), channel_id=1, source_target_pairs={{0,4},{4,8},{8,12},{1,5},{5,9},{9,13},{2,6},{6,10},{10,14},{3,7},{... | collective-permute-start | bytes 49160 | tf_op jit(solution)/shard_map/ppermute | solution.py:16
  13.2 5.6 %collective-permute-start.1 = (bf16[64,1,128]{2,0,1:T(8,128)(2,1)S(1)}, bf16[64,1,128]{2,0,1:T(8,128)(2,1)S(1)}, u32[]{:S(2)}, u32[]{:S(2)}) collective-permute-start(bf16[64,1,128]{2,0,1:T(8,128)(2,1)S(1)} %get-tuple-element.59), channel_id=1, source_target_pairs={{4,0},{8,4},{12,8},{5,1},{9,5},{13,9},{6,2},{10,6},{14,10},{7,3},{... | collective-permute-start | bytes 49160 | tf_op jit(solution)/shard_map/ppermute | solution.py:18
  18.9 4.4 %collective-permute-start.3 = (bf16[64,10,1]{2,0,1:T(8,128)(2,1)S(1)}, bf16[64,10,1]{2,0,1:T(8,128)(2,1)S(1)}, u32[]{:S(2)}, u32[]{:S(2)}) collective-permute-start(bf16[64,10,1]{2,0,1:T(8,128)(2,1)S(1)} %get-tuple-element.54), channel_id=1, source_target_pairs={{1,0},{2,1},{3,2},{5,4},{6,5},{7,6},{9,8},{10,9},{11,10},{13,12},{... | collective-permute-start | bytes 3848 | tf_op jit(solution)/shard_map/ppermute | solution.py:18
  20.2 4.0 %collective-permute-start.2 = (bf16[64,10,1]{2,0,1:T(8,128)(2,1)S(1)}, bf16[64,10,1]{2,0,1:T(8,128)(2,1)S(1)}, u32[]{:S(2)}, u32[]{:S(2)}) collective-permute-start(bf16[64,10,1]{2,0,1:T(8,128)(2,1)S(1)} %get-tuple-element.53), channel_id=1, source_target_pairs={{0,1},{1,2},{2,3},{4,5},{5,6},{6,7},{8,9},{9,10},{10,11},{12,13},{... | collective-permute-start | bytes 3848 | tf_op jit(solution)/shard_map/ppermute | solution.py:16
  24.7 0.9 copy-start.3
  24.8 0.9 copy-start.4
  28.0 6.4 %collective-permute-start.5 = (bf16[256,1,2]{1,0,2:T(8,128)(2,1)S(1)}, bf16[256,1,2]{1,0,2:T(8,128)(2,1)S(1)}, u32[]{:S(2)}, u32[]{:S(2)}) collective-permute-start(bf16[256,1,2]{1,0,2:T(8,128)(2,1)S(1)} %get-tuple-element.58), channel_id=1, source_target_pairs={{1,0},{2,1},{3,2},{5,4},{6,5},{7,6},{9,8},{10,9},{11,10},{13,12},{... | collective-permute-start | bytes 3080 | tf_op jit(solution)/shard_map/ppermute | solution.py:18
  29.3 5.8 %collective-permute-start.4 = (bf16[256,1,2]{1,0,2:T(8,128)(2,1)S(1)}, bf16[256,1,2]{1,0,2:T(8,128)(2,1)S(1)}, u32[]{:S(2)}, u32[]{:S(2)}) collective-permute-start(bf16[256,1,2]{1,0,2:T(8,128)(2,1)S(1)} %get-tuple-element.57), channel_id=1, source_target_pairs={{0,1},{1,2},{2,3},{4,5},{5,6},{6,7},{8,9},{9,10},{10,11},{12,13},{... | collective-permute-start | bytes 3080 | tf_op jit(solution)/shard_map/ppermute | solution.py:16
  49.2 1.0 copy-start.2
  53.0 4.0 %collective-permute-start.6 = (f32[256,1,8]{0,2,1:T(8,128)S(1)}, f32[256,1,8]{0,2,1:T(8,128)S(1)}, u32[]{:S(2)}, u32[]{:S(2)}) collective-permute-start(f32[256,1,8]{0,2,1:T(8,128)S(1)} %get-tuple-element.50), channel_id=1, source_target_pairs={{0,1},{1,2},{2,3},{4,5},{5,6},{6,7},{8,9},{9,10},{10,11},{12,13},{... | collective-permute-start | bytes 24584 | tf_op jit(solution)/shard_map/ppermute | solution.py:16
  55.7 7.9 %collective-permute-start.7 = (f32[256,1,8]{0,2,1:T(8,128)S(1)}, f32[256,1,8]{0,2,1:T(8,128)S(1)}, u32[]{:S(2)}, u32[]{:S(2)}) collective-permute-start(f32[256,1,8]{0,2,1:T(8,128)S(1)} %get-tuple-element.49), channel_id=1, source_target_pairs={{1,0},{2,1},{3,2},{5,4},{6,5},{7,6},{9,8},{10,9},{11,10},{13,12},{... | collective-permute-start | bytes 24584 | tf_op jit(solution)/shard_map/ppermute | solution.py:18
  64.4 72.1 %all-reduce.8.cloned.1.call-start = ((), (), s32[]{:S(2)}) async-start(), calls=%async_computation.3 | async-start | bytes 2949120 | tf_op jit(solution)/shard_map/psum | solution.py:110
  85.8 0.9 copy-start.1
  86.9 5.5 %collective-permute-start.8 = (bf16[64,1,128]{2,1,0:T(2,128)(2,1)S(1)}, bf16[64,1,128]{2,1,0:T(2,128)(2,1)S(1)}, u32[]{:S(2)}, u32[]{:S(2)}) collective-permute-start(bf16[64,1,128]{2,1,0:T(2,128)(2,1)S(1)} %get-tuple-element.56), channel_id=1, source_target_pairs={{0,4},{4,8},{8,12},{1,5},{5,9},{9,13},{2,6},{6,10},{10,14},{3,7},{... | collective-permute-start | bytes 49160 | tf_op jit(solution)/shard_map/ppermute | solution.py:16
  88.2 5.8 %collective-permute-start.9 = (bf16[64,1,128]{2,1,0:T(2,128)(2,1)S(1)}, bf16[64,1,128]{2,1,0:T(2,128)(2,1)S(1)}, u32[]{:S(2)}, u32[]{:S(2)}) collective-permute-start(bf16[64,1,128]{2,1,0:T(2,128)(2,1)S(1)} %get-tuple-element.55), channel_id=1, source_target_pairs={{4,0},{8,4},{12,8},{5,1},{9,5},{13,9},{6,2},{10,6},{14,10},{7,3},{... | collective-permute-start | bytes 49160 | tf_op jit(solution)/shard_map/ppermute | solution.py:18
  92.3 82.5 %all-reduce.6.cloned.1.call-start = ((), (), s32[]{:S(2)}) async-start(), calls=%async_computation.2 | async-start | bytes 589824 | tf_op jit(solution)/shard_map/psum | solution.py:110
  94.2 4.4 %collective-permute-start.11 = (bf16[64,10,1]{2,0,1:T(8,128)(2,1)S(1)}, bf16[64,10,1]{2,0,1:T(8,128)(2,1)S(1)}, u32[]{:S(2)}, u32[]{:S(2)}) collective-permute-start(bf16[64,10,1]{2,0,1:T(8,128)(2,1)S(1)} %get-tuple-element.52), channel_id=1, source_target_pairs={{1,0},{2,1},{3,2},{5,4},{6,5},{7,6},{9,8},{10,9},{11,10},{13,12},{... | collective-permute-start | bytes 3848 | tf_op jit(solution)/shard_map/ppermute | solution.py:18
  95.5 4.2 %collective-permute-start.10 = (bf16[64,10,1]{2,0,1:T(8,128)(2,1)S(1)}, bf16[64,10,1]{2,0,1:T(8,128)(2,1)S(1)}, u32[]{:S(2)}, u32[]{:S(2)}) collective-permute-start(bf16[64,10,1]{2,0,1:T(8,128)(2,1)S(1)} %get-tuple-element.51), channel_id=1, source_target_pairs={{0,1},{1,2},{2,3},{4,5},{5,6},{6,7},{8,9},{9,10},{10,11},{12,13},{... | collective-permute-start | bytes 3848 | tf_op jit(solution)/shard_map/ppermute | solution.py:16
Sparse Core Ops, SparseCore 0:
  64.5 20.1 reduce-scatter.1
  92.4 43.9 all-reduce.7
  138.8 35.9 all-reduce.5
